TPU v7x, 32 devices: a whole 2x2x4 slice. The times are simulated.
32 devices in a mesh: freq: 8 (over z, core), tile: 4 (over y, x).
Axes of the slice: x: 2, y: 2, z: 4, core: 2. Of those that a mesh axis runs over, the one named last changes fastest.
Arguments:
- recorded_seismograms: bfloat16 [2048, 16, 2048], P('freq', None, 'tile'), may hold values from -6 to 6
- left_bases: bfloat16 [8, 64, 8, 2, 32, 256], P('freq', None, 'tile'), may hold values from -1 to 1
- right_bases: bfloat16 [8, 64, 8, 2, 32, 256], P('freq', None, 'tile'), may hold values from -0.125 to 0.125
- rank_classes: int32 [8, 64, 8], P('freq', None, 'tile'), may hold values from 0 to 3
- owner: int32 [64], replicated, may hold values from 0 to 63, each once
Outputs:
- echo: float32 [8, 64, 2, 16, 256], P('freq', 'tile')
- adjoint_traces: bfloat16 [2048, 16, 2048], P('freq', None, 'tile')
Inputs may be any that keep to these rules, and one draw needn't show every extreme that they name: `rank_classes`: rank class of a tile, 0 to 3. `owner`: each row tile stands at exactly one position.
All inputs are finite; a program needn't handle non-finite values.
Results may differ from a plain program's by a relative error of at most 0.03.
Values may be sent and summed in bfloat16 or wider, within the bound.
A program may use at most 128 MiB of HBM per device.

v0:
```python
import math

import jax
import jax.numpy as jnp
from jax import lax
from jax.sharding import PartitionSpec as P

TILE = 256
RMAX = 32
S = 16
RECORD_LENGTH = 2048
LOW_BIN = 8


def fourier_kernel_matrices(spectral_bins, recording_moments):
    dyadic_matrix = spectral_bins[:, None] * recording_moments[None, :] % RECORD_LENGTH
    angles = dyadic_matrix.astype(jnp.float32) * (2.0 * math.pi / RECORD_LENGTH)
    return (jnp.cos(angles), jnp.sin(angles))


def contract(form, first, second):
    return jnp.einsum(form, first, second, preferred_element_type=jnp.float32)


def seismogram_fourier_coeffs(seismogram_amplitudes, spectral_bins, recording_moments):
    count = seismogram_amplitudes.shape[0]
    columns = seismogram_amplitudes.shape[2]
    flat = seismogram_amplitudes.astype(jnp.float32).reshape(count, -1)
    cosinusoid_entries, sinusoid_matrix = fourier_kernel_matrices(spectral_bins, recording_moments)
    highest = lax.Precision.HIGHEST
    real_part = jnp.dot(cosinusoid_entries, flat, precision=highest) * RECORD_LENGTH ** (-0.5)
    imag_part = -jnp.dot(sinusoid_matrix, flat, precision=highest) * RECORD_LENGTH ** (-0.5)
    return jnp.stack([real_part, imag_part], 1).reshape(spectral_bins.shape[0], 2, S, columns)


def shards(recorded_seismograms, left_bases, right_bases, rank_classes, owner):
    n_freq = lax.axis_size("freq")
    device_clock_grid = recorded_seismograms.shape[0]
    local_cols = recorded_seismograms.shape[2]
    per_device = left_bases.shape[0]
    col_tiles = left_bases.shape[2]
    freq_total = per_device * n_freq
    recording_moments = lax.axis_index("freq") * device_clock_grid + jnp.arange(
        device_clock_grid, dtype=jnp.int32
    )
    spectral_bins = (
        LOW_BIN + jnp.int32(0) + jnp.arange(per_device * lax.axis_size("freq"), dtype=jnp.int32)
    )
    spectra = lax.psum_scatter(
        seismogram_fourier_coeffs(recorded_seismograms, spectral_bins, recording_moments).astype(
            jnp.bfloat16
        ),
        "freq",
        scatter_dimension=0,
        tiled=True,
    )
    spectra = spectra.reshape(per_device, 2, S, col_tiles, TILE)
    limits = (rank_classes + 1) * (RMAX // 4)
    kept = (jnp.arange(RMAX, dtype=jnp.int32)[None, None, None, :] < limits[..., None]).astype(
        jnp.float32
    )[..., None]
    left_real, left_imag = (left_bases[:, :, :, 0], left_bases[:, :, :, 1])
    right_real, right_imag = (right_bases[:, :, :, 0], right_bases[:, :, :, 1])
    spec_real, spec_imag = (spectra[:, 0], spectra[:, 1])
    fwd_real = contract("fijrt,fsjt->fijrs", right_real, spec_real) - contract(
        "fijrt,fsjt->fijrs", right_imag, spec_imag
    )
    fwd_imag = contract("fijrt,fsjt->fijrs", right_real, spec_imag) + contract(
        "fijrt,fsjt->fijrs", right_imag, spec_real
    )
    fwd_real = (fwd_real * kept).astype(jnp.bfloat16)
    fwd_imag = (fwd_imag * kept).astype(jnp.bfloat16)
    out_real = contract("fijrt,fijrs->fist", left_real, fwd_real) - contract(
        "fijrt,fijrs->fist", left_imag, fwd_imag
    )
    out_imag = contract("fijrt,fijrs->fist", left_real, fwd_imag) + contract(
        "fijrt,fijrs->fist", left_imag, fwd_real
    )
    partial_rows = jnp.take(jnp.stack([out_real, out_imag], 2), owner, axis=1)
    echo = lax.psum_scatter(
        partial_rows.astype(jnp.bfloat16), "tile", scatter_dimension=1, tiled=True
    ).astype(jnp.float32)
    piece = lax.all_gather(echo.astype(jnp.bfloat16), "tile", axis=1, tiled=True)
    left_piece = jnp.take(left_bases, owner, axis=1)
    right_piece = jnp.take(right_bases, owner, axis=1)
    kept_piece = jnp.take(kept, owner, axis=1)
    piece_left_real = left_piece[:, :, :, 0]
    piece_left_imag = left_piece[:, :, :, 1]
    piece_right_real = right_piece[:, :, :, 0]
    piece_right_imag = right_piece[:, :, :, 1]
    rows_real = piece[:, :, 0]
    rows_imag = piece[:, :, 1]
    adj_real = contract("fijrt,fist->fijrs", piece_left_real, rows_real) + contract(
        "fijrt,fist->fijrs", piece_left_imag, rows_imag
    )
    adj_imag = contract("fijrt,fist->fijrs", piece_left_real, rows_imag) - contract(
        "fijrt,fist->fijrs", piece_left_imag, rows_real
    )
    adj_real = (adj_real * kept_piece).astype(jnp.bfloat16)
    adj_imag = (adj_imag * kept_piece).astype(jnp.bfloat16)
    col_real = contract("fijrt,fijrs->fsjt", piece_right_real, adj_real) + contract(
        "fijrt,fijrs->fsjt", piece_right_imag, adj_imag
    )
    col_imag = contract("fijrt,fijrs->fsjt", piece_right_real, adj_imag) - contract(
        "fijrt,fijrs->fsjt", piece_right_imag, adj_real
    )
    adjoint = jnp.stack([col_real, col_imag], 1)
    adjoint = adjoint.reshape(per_device, 2, S, local_cols).astype(jnp.bfloat16)
    piece = lax.all_gather(adjoint, "freq", axis=0, tiled=True)
    count = piece.shape[0]
    spectral_bins = LOW_BIN + jnp.int32(0) + jnp.arange(count, dtype=jnp.int32)
    cosinusoid_entries, sinusoid_matrix = fourier_kernel_matrices(spectral_bins, recording_moments)
    values = piece.astype(jnp.float32)
    highest = lax.Precision.HIGHEST
    added = jnp.einsum("ft,fsc->tsc", cosinusoid_entries, values[:, 0], precision=highest)
    added = added - jnp.einsum("ft,fsc->tsc", sinusoid_matrix, values[:, 1], precision=highest)
    synth = added * freq_total ** (-0.5)
    return (echo, synth.astype(jnp.bfloat16))


def solution(mesh):
    in_specs = (
        P("freq", None, "tile"),
        P("freq", None, "tile", None, None, None),
        P("freq", None, "tile", None, None, None),
        P("freq", None, "tile"),
        P(),
    )
    out_specs = (P("freq", "tile", None, None, None), P("freq", None, "tile"))
    return jax.shard_map(shards, mesh=mesh, in_specs=in_specs, out_specs=out_specs, check_vma=False)
```

profile of v0, /device:TPU:0, one launch (start us, length us, event | category | flops | bytes accessed | tf_op | source)
XLA Modules:
  0.0 170.9 jit_solution(5736225025213706652)
XLA Ops:
  7.2 0.0 reduce-scatter.3.cloned.1.call-start
  7.2 6.5 %copy.106 = bf16[32,8,16,512]{3,1,2,0:T(8,128)(2,1)S(1)} copy(bf16[32,8,16,512]{3,2,1,0:T(8,128)(2,1)} %bitcast.267) | data formatting | bytes 8388608
  13.7 0.0 copy-start.7
  13.7 0.0 copy-start.5
  13.8 1.8 %fusion.2 = bf16[8,8192]{1,0:T(8,128)(2,1)S(1)} fusion(bf16[256,8192]{1,0:T(8,128)(2,1)S(1)} %bitcast.264, s32[256]{0:T(256)S(1)} %iota_add_fusion, s32[8]{0:T(128)S(1)} %iota_add_fusion.1), kind=kOutput, calls=%fused_computation.8 | convolution fusion | flops 201551872 | bytes 4326432 | tf_op jit(solution)/shard_map/dot_general | solution.py:32
  15.6 1.8 %fusion.1 = bf16[8,8192]{1,0:T(8,128)(2,1)S(1)} fusion(bf16[256,8192]{1,0:T(8,128)(2,1)S(1)} %bitcast.265, s32[256]{0:T(256)S(1)} %iota_add_fusion, s32[8]{0:T(128)S(1)} %iota_add_fusion.1), kind=kOutput, calls=%fused_computation.7 | convolution fusion | flops 201486336 | bytes 4326432 | tf_op jit(solution)/shard_map/dot_general | solution.py:31
  17.5 0.7 pad_maximum_fusion
  18.3 0.0 reduce-scatter.3.cloned.1.call-update
  18.3 0.2 reduce-scatter.5.cloned.1.call-start
  18.5 0.0 copy-done.7
  18.5 0.0 copy-done.5
  18.6 4.2 %fusion.107 = (bf16[1,64,2,1,32,256]{5,4,3,2,1,0:T(8,128)(2,1)}, bf16[1,64,2,1,32,256]{5,4,3,2,1,0:T(8,128)(2,1)S(1)}) fusion(bf16[1,64,2,2,32,256]{5,4,3,2,1,0:T(8,128)(2,1)} %param.9), kind=kLoop, calls=%fused_computation.127 | loop fusion | bytes 8388608 | tf_op jit(solution)/shard_map/slice | solution.py:63
  22.8 28.6 %reduce-scatter.3.cloned.1.call-done = bf16[1,2,16,512]{3,2,1,0:T(8,128)(2,1)} async-done(((bf16[8,2,16,512]{3,2,1,0:T(8,128)(2,1)}), bf16[1,2,16,512]{3,2,1,0:T(8,128)(2,1)}) %reduce-scatter.3.cloned.1.call-update) | async-done | bytes 32784 | tf_op jit(solution)/shard_map/reduce_scatter | solution.py:49
  51.4 0.8 reshape.241
  52.2 0.0 copy-start.1
  52.3 2.3 %fusion.12 = f32[2,16,64,32]{2,1,3,0:T(8,128)S(1)} fusion(bf16[1,64,2,1,32,256]{5,4,3,2,1,0:T(8,128)(2,1)S(1)} %get-tuple-element.12, bf16[1,1,16,2,256]{4,3,2,1,0:T(2,128)(2,1)S(1)} %get-tuple-element.16), kind=kOutput, calls=%fused_computation.29 | convolution fusion | flops 33554432 | bytes 2375680 | tf_op jit(solution)/shard_map/fijrt,fsjt->fijrs/dot_general | solution.py:22
  54.6 2.3 %fusion.13 = f32[2,16,64,32]{2,1,3,0:T(8,128)S(1)} fusion(bf16[1,64,2,1,32,256]{5,4,3,2,1,0:T(8,128)(2,1)S(1)} %get-tuple-element.12, bf16[1,1,16,2,256]{4,3,2,1,0:T(2,128)(2,1)S(1)} %get-tuple-element.15), kind=kOutput, calls=%fused_computation.30 | convolution fusion | flops 33554432 | bytes 2375680 | tf_op jit(solution)/shard_map/fijrt,fsjt->fijrs/dot_general | solution.py:22
  56.9 0.0 copy-done.1
  56.9 2.4 %fusion.66 = bf16[64,2,32,16]{0,3,2,1:T(8,128)(2,1)S(1)} fusion(f32[2,16,64,32]{2,1,3,0:T(8,128)S(1)} %fusion.12, bf16[1,64,2,1,32,256]{5,4,3,2,1,0:T(8,128)(2,1)S(1)} %copy-done.1, f32[64,2,32]{0,2,1:T(8,128)S(1)} %fusion.79, bf16[1,1,16,2,256]{4,3,2,1,0:T(2,128)(2,1)S(1)} %get-tuple-element.15), kind=kOutput, calls=%fused_computation.67 | convolution fusion | flops 33751040 | bytes 2523136 | tf_op jit(solution)/shard_map/fijrt,fsjt->fijrs/dot_general | solution.py:22
  59.2 2.4 %fusion.67 = bf16[64,2,32,16]{0,3,2,1:T(8,128)(2,1)S(1)} fusion(f32[2,16,64,32]{2,1,3,0:T(8,128)S(1)} %fusion.13, bf16[1,64,2,1,32,256]{5,4,3,2,1,0:T(8,128)(2,1)S(1)} %copy-done.1, f32[64,2,32]{0,2,1:T(8,128)S(1)} %fusion.79, bf16[1,1,16,2,256]{4,3,2,1,0:T(2,128)(2,1)S(1)} %get-tuple-element.16), kind=kOutput, calls=%fused_computation.68 | convolution fusion | flops 33751040 | bytes 2523136 | tf_op jit(solution)/shard_map/fijrt,fsjt->fijrs/dot_general | solution.py:22
  61.6 0.9 copy.72
  62.5 0.9 copy.74
  63.4 0.0 copy-start
  63.4 2.2 %fusion.31 = f32[64,16,256]{2,1,0:T(8,128)S(1)} fusion(bf16[64,2,32,16]{2,3,1,0:T(8,128)(2,1)S(1)} %copy.74, bf16[1,64,2,2,32,256]{5,4,3,2,1,0:T(8,128)(2,1)} %param.8), kind=kOutput, calls=%fused_computation.46 | convolution fusion | flops 33554432 | bytes 3276800 | tf_op jit(solution)/shard_map/fijrt,fijrs->fist/dot_general | solution.py:22
  65.6 2.3 %fusion.28 = f32[64,16,256]{2,1,0:T(8,128)S(1)} fusion(bf16[64,2,32,16]{2,3,1,0:T(8,128)(2,1)S(1)} %copy.72, bf16[1,64,2,2,32,256]{5,4,3,2,1,0:T(8,128)(2,1)} %param.8), kind=kOutput, calls=%fused_computation.45 | convolution fusion | flops 33554432 | bytes 3276800 | tf_op jit(solution)/shard_map/fijrt,fijrs->fist/dot_general | solution.py:22
  67.9 0.0 copy-done
  67.9 0.5 fusion.47
  68.4 0.5 fusion.53
  68.9 0.1 maximum_bitcast_fusion
  69.0 0.6 gather_fusion
  69.6 1.2 fusion.11
  70.8 0.0 reduce-scatter.5.cloned.1.call-update
  70.9 0.0 all-gather.2.cloned.1.call-start
  70.9 26.0 %reduce-scatter.5.cloned.1.call-done = bf16[1,16,2,16,256]{4,3,2,1,0:T(8,128)(2,1)} async-done(((bf16[1,64,2,16,256]{4,3,2,1,0:T(8,128)(2,1)}), bf16[1,16,2,16,256]{4,3,2,1,0:T(8,128)(2,1)}) %reduce-scatter.5.cloned.1.call-update) | async-done | bytes 262160 | tf_op jit(solution)/shard_map/reduce_scatter | solution.py:80
  96.9 0.0 all-gather.2.cloned.1.call-update
  97.0 0.1 copy.81
  97.1 0.7 gather_fusion.1
  97.7 5.0 %gather_fusion.3 = bf16[64,2,2,32,256]{4,3,2,1,0:T(8,128)(2,1)} fusion(bf16[64,2,2,32,256]{4,3,2,1,0:T(8,128)(2,1)} %bitcast.266, s32[1024]{0:T(1024)S(1)} %pad_clamp_fusion), kind=kCustom, calls=%fused_computation.1.clone | custom fusion | bytes 8388864 | tf_op jit(solution)/shard_map/jit(_take)/gather | solution.py:85
  102.7 5.0 %gather_fusion.2 = bf16[64,2,2,32,256]{4,3,2,1,0:T(8,128)(2,1)} fusion(bf16[64,2,2,32,256]{4,3,2,1,0:T(8,128)(2,1)} %bitcast.263, s32[1024]{0:T(1024)S(1)} %pad_clamp_fusion), kind=kCustom, calls=%fused_computation.clone | custom fusion | bytes 8388864 | tf_op jit(solution)/shard_map/jit(_take)/gather | solution.py:84
  107.7 0.1 broadcast_select_fusion
  107.8 0.0 copy-start.4
  107.9 6.1 %bitcast_select_fusion = (bf16[1,64,2,2,32,256]{5,4,2,1,3,0:T(8,128)(2,1)}, bf16[1,64,2,2,32,256]{5,4,2,1,3,0:T(8,128)(2,1)}) fusion(bf16[64,2,2,32,256]{4,3,2,1,0:T(8,128)(2,1)} %gather_fusion.3, pred[64]{0:T(512)(128)(4,1)S(1)} %compare_and_fusion, bf16[64,2,2,32,256]{4,3,2,1,0:T(8,128)(2,1)} %gather_fusion.2), kind=kLoop, calls=%fused_computation.10 | loop fusion | flops 4194304 | bytes 16777280 | tf_op jit(solution)/shard_map/jit(_take)/select_n | solution.py:85
  113.9 0.0 copy-done.4
  113.9 0.8 convert_element_type.68
  114.8 10.7 %all-gather.2.cloned.1.call-done = bf16[1,64,2,16,256]{4,3,2,0,1:T(8,128)(2,1)} async-done(((bf16[1,16,2,16,256]{4,3,2,0,1:T(8,128)(2,1)}), bf16[1,64,2,16,256]{4,3,2,0,1:T(8,128)(2,1)}) %all-gather.2.cloned.1.call-update) | async-done | bytes 1048592 | tf_op jit(solution)/shard_map/all_gather | solution.py:83
  125.4 0.0 copy-start.2
  125.4 3.3 %fusion.16 = f32[64,2,32,16]{2,3,1,0:T(8,128)S(1)} fusion(bf16[1,64,2,2,32,256]{5,4,2,1,3,0:T(8,128)(2,1)} %get-tuple-element.18, bf16[1,64,2,16,256]{4,3,2,0,1:T(8,128)(2,1)} %all-gather.2.cloned.1.call-done), kind=kOutput, calls=%fused_computation.33 | convolution fusion | flops 33554432 | bytes 2883584 | tf_op jit(solution)/shard_map/fijrt,fist->fijrs/dot_general | solution.py:22
  128.7 0.0 copy-start.3
  128.7 0.0 copy-start.6
  128.7 3.3 %fusion.56 = bf16[64,2,32,16]{2,3,1,0:T(8,128)(2,1)S(1)} fusion(f32[64,2,32,16]{2,3,1,0:T(8,128)S(1)} %fusion.16, bf16[1,64,2,2,32,256]{5,4,2,1,3,0:T(8,128)(2,1)} %get-tuple-element.18, f32[64,2,32]{2,1,0:T(2,128)S(1)} %broadcast_select_fusion, bf16[1,64,2,16,256]{4,3,2,0,1:T(8,128)(2,1)} %all-gather.2.cloned.1.call-done), kind=kOutput, calls=%fused_computation.57 | convolution fusion | flops 33751040 | bytes 3031040 | tf_op jit(solution)/shard_map/fijrt,fist->fijrs/dot_general | solution.py:22
  132.1 0.0 copy-done.2
  132.1 0.5 fusion.68
  132.6 0.0 copy-done.3
  132.6 0.0 copy-done.6
  132.6 1.5 fusion.17
  134.1 1.5 fusion.57
  135.5 0.5 fusion.69
  136.0 0.5 fusion.77
  136.5 0.5 fusion.76
  137.1 14.5 %all_gather.7 = bf16[8,2,16,512]{3,2,1,0:T(8,128)(2,1)S(1)} all-gather(bf16[1,2,16,512]{3,2,1,0:T(8,128)(2,1)S(1)} %pad_maximum_fusion.1), channel_id=1, replica_groups=mesh['freq'=8,'tile'=4] {'freq'}, dimensions={0}, use_global_device_ids=true | all-gather | bytes 294912 | tf_op jit(solution)/shard_map/all_gather | solution.py:109
  151.7 3.6 %fusion.78 = f32[256,16,512]{2,0,1:T(8,128)S(1)} fusion(bf16[8,1,16,512]{3,2,1,0:T(8,128)(2,1)S(1)} %get-tuple-element.14, s32[256]{0:T(256)S(1)} %iota_add_fusion, s32[8]{0:T(128)S(1)} %iota_add_fusion.1), kind=kOutput, calls=%fused_computation.84 | convolution fusion | flops 201355264 | bytes 8520736 | tf_op jit(solution)/shard_map/ft,fsc->tsc/dot_general | solution.py:115
  155.3 4.7 %multiply_convert_fusion = bf16[256,16,512]{2,0,1:T(8,128)(2,1)S(1)} fusion(f32[256,16,512]{2,0,1:T(8,128)S(1)} %fusion.78, bf16[8,1,16,512]{3,2,1,0:T(8,128)(2,1)S(1)} %get-tuple-element.13, s32[256]{0:T(256)S(1)} %iota_add_fusion, s32[8]{0:T(128)S(1)} %iota_add_fusion.1), kind=kOutput, calls=%fused_computation.9 | convolution fusion | flops 207646720 | bytes 12715040 | tf_op jit(solution)/shard_map/ft,fsc->tsc/dot_general | solution.py:116
  160.0 4.4 %copy.87 = bf16[256,16,512]{2,1,0:T(8,128)(2,1)} copy(bf16[256,16,512]{2,0,1:T(8,128)(2,1)S(1)} %multiply_convert_fusion) | data formatting | bytes 8388608
  (17 shorter events, 0.3 us)
Async XLA Ops:
  7.2 44.3 %reduce-scatter.3.cloned.1.call-start = ((), (), s32[]{:S(2)}) async-start(), calls=%async_computation.2 | async-start | bytes 294912 | tf_op jit(solution)/shard_map/reduce_scatter | solution.py:49
  13.7 4.8 %copy-start.7 = (s32[64]{0:T(128)S(1)}, s32[64]{0:T(128)}, u32[]{:S(2)}) copy-start(s32[64]{0:T(128)} %param.11) | copy-start | bytes 772
  13.7 4.8 %copy-start.5 = (s32[1,64,2]{1,2,0:T(2,128)S(1)}, s32[1,64,2]{1,2,0:T(2,128)}, u32[]{:S(2)}) copy-start(s32[1,64,2]{1,2,0:T(2,128)} %param.10) | copy-start | bytes 1540
  18.3 78.7 %reduce-scatter.5.cloned.1.call-start = ((), (), s32[]{:S(2)}) async-start(), calls=%async_computation.3 | async-start | bytes 1310720 | tf_op jit(solution)/shard_map/reduce_scatter | solution.py:80
  52.2 4.6 %copy-start.1 = (bf16[1,64,2,1,32,256]{5,4,3,2,1,0:T(8,128)(2,1)S(1)}, bf16[1,64,2,1,32,256]{5,4,3,2,1,0:T(8,128)(2,1)}, u32[]{:S(2)}) copy-start(bf16[1,64,2,1,32,256]{5,4,3,2,1,0:T(8,128)(2,1)} %get-tuple-element.11) | copy-start | bytes 6291460
  63.4 4.5 %copy-start = (bf16[1,64,2,2,32,256]{5,4,3,2,1,0:T(8,128)(2,1)S(1)}, bf16[1,64,2,2,32,256]{5,4,3,2,1,0:T(8,128)(2,1)}, u32[]{:S(2)}) copy-start(bf16[1,64,2,2,32,256]{5,4,3,2,1,0:T(8,128)(2,1)} %param.8) | copy-start | bytes 12582916
  70.9 54.6 %all-gather.2.cloned.1.call-start = ((), (), s32[]{:S(2)}) async-start(), calls=%async_computation.4 | async-start | bytes 1310720 | tf_op jit(solution)/shard_map/all_gather | solution.py:83
  107.8 6.1 %copy-start.4 = (bf16[1,16,2,16,256]{4,3,2,1,0:T(8,128)(2,1)S(1)}, bf16[1,16,2,16,256]{4,3,2,1,0:T(8,128)(2,1)}, u32[]{:S(2)}) copy-start(bf16[1,16,2,16,256]{4,3,2,1,0:T(8,128)(2,1)} %reduce-scatter.5.cloned.1.call-done) | copy-start | bytes 786436
  125.4 6.6 %copy-start.2 = (bf16[1,64,2,2,32,256]{5,4,2,1,3,0:T(8,128)(2,1)S(1)}, bf16[1,64,2,2,32,256]{5,4,2,1,3,0:T(8,128)(2,1)}, u32[]{:S(2)}) copy-start(bf16[1,64,2,2,32,256]{5,4,2,1,3,0:T(8,128)(2,1)} %get-tuple-element.17) | copy-start | bytes 12582916
  128.7 3.8 %copy-start.3 = (bf16[1,64,2,2,32,256]{5,4,2,1,3,0:T(8,128)(2,1)S(1)}, bf16[1,64,2,2,32,256]{5,4,2,1,3,0:T(8,128)(2,1)}, u32[]{:S(2)}) copy-start(bf16[1,64,2,2,32,256]{5,4,2,1,3,0:T(8,128)(2,1)} %get-tuple-element.18) | copy-start | bytes 12582916
  128.7 3.8 %copy-start.6 = (bf16[1,64,2,16,256]{4,3,2,0,1:T(8,128)(2,1)S(1)}, bf16[1,64,2,16,256]{4,3,2,0,1:T(8,128)(2,1)}, u32[]{:S(2)}) copy-start(bf16[1,64,2,16,256]{4,3,2,0,1:T(8,128)(2,1)} %all-gather.2.cloned.1.call-done) | copy-start | bytes 3145732
Sparse Core Ops, SparseCore 0:
  18.4 32.9 reduce-scatter.2
  71.0 25.9 reduce-scatter.4
  98.8 26.6 all-gather.1
where the time goes:
time: 171 us
  waiting for transfers between devices  65.4 us (38%)
  matrix products  38.3 us (22%)
  local copies, waits for them, and re-layouts  29.3 us (17%)
  blocking collectives  14.5 us (8%)
  between operations  14 us (8%)
  other arithmetic  9.13 us (5%)
    reduce_scatter x1, waiting for transfers between devices, shards(): lax.psum_scatter(seismogram_fourier_coeffs(recorded_seismograms, spectral...  28.6 us
    dot_general x16, matrix products, contract(): return jnp.einsum(form, first, second, preferred_element_type=jnp.float32)  26.3 us
    reduce_scatter x1, waiting for transfers between devices, shards(): lax.psum_scatter(partial_rows.astype(jnp.bfloat16), 'tile', scatter_dimen...  26 us
    all_gather x1, blocking collectives, shards(): piece = lax.all_gather(adjoint, 'freq', axis=0, tiled=True)  14.5 us
    unnamed x18, local copies, waits for them, and re-layouts  10.9 us
    all_gather x1, waiting for transfers between devices, shards(): lax.all_gather(echo.astype(jnp.bfloat16), 'tile', axis=1, tiled=True)  10.7 us
    select_n x1, other arithmetic, shards(): right_piece = jnp.take(right_bases, owner, axis=1)  6.05 us
    gather x1, local copies, waits for them, and re-layouts, shards(): right_piece = jnp.take(right_bases, owner, axis=1)  5.02 us
  transfers between devices with their start and end apart: 3, of which 3 were waited for; matrix products, arithmetic and copies ran while one was open for 13% of the time, Pallas kernels for 0%

commit v1 on v0

v1 whole, which is shorter than its diff:
```python
import functools
import math

import jax
import jax.numpy as jnp
import numpy as np
from jax import lax
from jax.experimental import pallas as pl
from jax.experimental.pallas import tpu as pltpu
from jax.sharding import PartitionSpec as P

TILE = 256
RMAX = 32
S = 16
RECORD_LENGTH = 2048
LOW_BIN = 8
GROUP = 4
F32 = jnp.float32
BF16 = jnp.bfloat16
MESH = pl.DeviceIdType.MESH


def trig_tables(shards, count, freqs):
    bins = LOW_BIN + np.arange(freqs)
    angles = (bins[:, None] * np.arange(shards * count)[None, :] % RECORD_LENGTH) * (
        2.0 * math.pi / RECORD_LENGTH
    )
    both = np.stack([np.cos(angles), -np.sin(angles)], 1)
    both = both.reshape(2 * freqs, shards, count)
    ahead = np.repeat(both.transpose(1, 0, 2), S, axis=2)
    back = np.repeat(both.transpose(1, 2, 0), S, axis=2)
    return jnp.asarray(ahead, BF16), jnp.asarray(back, BF16)


def partner(me, off, size):
    out = me
    bit = 1
    while bit < size:
        if off & bit:
            out = out + (1 - 2 * ((me // bit) % 2)) * bit
        bit *= 2
    return out


def nt_dot(a, b):
    return lax.dot_general(a, b, (((1,), (1,)), ((), ())), preferred_element_type=F32)


def nn_dot(a, b):
    return jnp.dot(a, b, preferred_element_type=F32)


def apply_kernel(
    nf,
    nt,
    x_hbm,
    l_hbm,
    r_hbm,
    rank_ref,
    owner_ref,
    ahead_hbm,
    echo_ref,
    spec_out,
    x_ref,
    l_ref,
    r_ref,
    ahead_ref,
    a_ref,
    acc_ref,
    part_ref,
    rs_ref,
    s_ref,
    send_ref,
    recv_ref,
    own_ref,
    rows_ref,
    adj_ref,
    gath_ref,
    load_sem,
    rs_send,
    rs_recv,
    row_send,
    row_recv,
    ag_send,
    ag_recv,
    sp_send,
    sp_recv,
):
    me_f = lax.axis_index("freq")
    me_t = lax.axis_index("tile")
    count = x_ref.shape[0]
    cols = x_ref.shape[2]
    col_tiles = l_ref.shape[1]
    freqs = part_ref.shape[0]
    npos = own_ref.shape[0]
    quads = npos // GROUP
    chunks = 4
    step_t = count // chunks
    kk = step_t * S

    ahead_copy = pltpu.make_async_copy(ahead_hbm.at[me_f], ahead_ref, load_sem.at[0])
    ahead_copy.start()
    x_copies = []
    for n in range(chunks):
        cp = pltpu.make_async_copy(
            x_hbm.at[pl.ds(n * step_t, step_t)], x_ref.at[pl.ds(n * step_t, step_t)], load_sem.at[1 + n]
        )
        cp.start()
        x_copies.append(cp)
    r_copy = pltpu.make_async_copy(r_hbm, r_ref, load_sem.at[1 + chunks])
    r_copy.start()
    l_copy = pltpu.make_async_copy(l_hbm, l_ref, load_sem.at[2 + chunks])
    l_copy.start()

    barrier = pltpu.get_barrier_semaphore()
    for off in range(1, nf):
        pl.semaphore_signal(
            barrier, inc=1, device_id=(partner(me_f, off, nf), me_t), device_id_type=MESH
        )
    for off in range(1, nt):
        pl.semaphore_signal(
            barrier, inc=1, device_id=(me_f, partner(me_t, off, nt)), device_id_type=MESH
        )

    ahead_copy.wait()
    diag = lax.broadcasted_iota(jnp.int32, (S, kk), 1) % S == lax.broadcasted_iota(
        jnp.int32, (S, kk), 0
    )
    for n in range(chunks):
        table = ahead_ref[:, n * kk : (n + 1) * kk].astype(F32)
        for k in range(2 * freqs):
            row = jnp.broadcast_to(table[k : k + 1], (S, kk))
            a_ref[k * S : (k + 1) * S, n * kk : (n + 1) * kk] = jnp.where(diag, row, 0.0).astype(
                BF16
            )
    for n in range(chunks):
        x_copies[n].wait()
    total = nn_dot(a_ref[...], x_ref[...].reshape(count * S, cols)) * RECORD_LENGTH**-0.5
    total = total.reshape(freqs, 2 * S, cols)
    acc_ref[...] = total
    part_ref[...] = total.astype(BF16)

    pl.semaphore_wait(barrier, nf + nt - 2)
    rs_copies = []
    for off in range(nf - 1, 0, -1):
        to = partner(me_f, off, nf)
        cp = pltpu.make_async_remote_copy(
            src_ref=part_ref.at[to],
            dst_ref=rs_ref.at[off],
            send_sem=rs_send.at[off],
            recv_sem=rs_recv.at[off],
            device_id=(to, me_t),
            device_id_type=MESH,
        )
        cp.start()
        rs_copies.append((off, cp))
    adj_ref[...] = jnp.zeros_like(adj_ref)
    r_copy.wait()
    l_copy.wait()
    spectra = acc_ref[me_f]
    for off, cp in rs_copies:
        cp.wait()
        spectra = spectra + rs_ref[off].astype(F32)
    s_ref[...] = spectra.astype(BF16)

    width = GROUP * RMAX
    lane = lax.broadcasted_iota(jnp.int32, (1, width), 1)
    lane_m = lane // RMAX
    lane_r = lane % RMAX
    block = (
        lax.broadcasted_iota(jnp.int32, (GROUP * 2 * S, width), 0) // (2 * S)
        == lax.broadcasted_iota(jnp.int32, (GROUP * 2 * S, width), 1) // RMAX
    )

    def gather(ref, idx, j, c):
        return [ref[i, j, c] for i in idx]

    def kept(idx, j):
        limit = jnp.zeros((1, width), jnp.int32)
        for m, i in enumerate(idx):
            value = (rank_ref[i * col_tiles + j] + 1) * (RMAX // 4)
            limit = jnp.where(lane_m == m, value, limit)
        return jnp.where(lane_r < limit, 1.0, 0.0).astype(F32)

    def forward(base):
        idx = [owner_ref[base + m] for m in range(GROUP)]
        left, weights = [], []
        for j in range(col_tiles):
            right = jnp.concatenate(gather(r_ref, idx, j, 0) + gather(r_ref, idx, j, 1), 0)
            p = nt_dot(s_ref[:, j * TILE : (j + 1) * TILE], right)
            keep = kept(idx, j)
            wr = (p[:S, :width] - p[S:, width:]) * keep
            wi = (p[S:, :width] + p[:S, width:]) * keep
            for first in ([wr, wi], [-wi, wr]):
                tiled = jnp.concatenate(first * GROUP, 0)
                weights.append(jnp.where(block, tiled, 0.0).astype(BF16))
            left += gather(l_ref, idx, j, 0) + gather(l_ref, idx, j, 1)
        return nn_dot(jnp.concatenate(weights, 1), jnp.concatenate(left, 0))

    def backward(base, rows):
        idx = [owner_ref[base + m] for m in range(GROUP)]
        left = []
        for j in range(col_tiles):
            left += gather(l_ref, idx, j, 0) + gather(l_ref, idx, j, 1)
        p = nt_dot(rows, jnp.concatenate(left, 0))
        for j in range(col_tiles):
            sums = []
            for c in range(2):
                at = (2 * j + c) * width
                q = jnp.where(block, p[:, at : at + width], 0.0)
                g = q[: 2 * S]
                for m in range(1, GROUP):
                    g = g + q[2 * S * m : 2 * S * (m + 1)]
                sums.append(g)
            keep = kept(idx, j)
            ar = (sums[0][:S] + sums[1][S:]) * keep
            ai = (sums[0][S:] - sums[1][:S]) * keep
            lhs = jnp.concatenate(
                [jnp.concatenate([ar, ai], 0), jnp.concatenate([ai, -ar], 0)], 1
            ).astype(BF16)
            right = jnp.concatenate(gather(r_ref, idx, j, 0) + gather(r_ref, idx, j, 1), 0)
            adj_ref[:, j * TILE : (j + 1) * TILE] += nn_dot(lhs, right)

    def row_copy(off, q):
        return pltpu.make_async_remote_copy(
            src_ref=send_ref.at[off - 1, q],
            dst_ref=recv_ref.at[off - 1, q],
            send_sem=row_send.at[off - 1, q],
            recv_sem=row_recv.at[off - 1, q],
            device_id=(me_f, partner(me_t, off, nt)),
            device_id_type=MESH,
        )

    def rows_copy(off, q):
        return pltpu.make_async_remote_copy(
            src_ref=rows_ref.at[0, q],
            dst_ref=rows_ref.at[off, q],
            send_sem=ag_send.at[off - 1, q],
            recv_sem=ag_recv.at[off - 1, q],
            device_id=(me_f, partner(me_t, off, nt)),
            device_id_type=MESH,
        )

    @pl.loop(0, quads)
    def _(q):
        for off in range(nt - 1, 0, -1):
            out = forward(partner(me_t, off, nt) * npos + q * GROUP)
            send_ref[off - 1, q] = out.astype(BF16)
            row_copy(off, q).start()
        out = forward(me_t * npos + q * GROUP)
        own_ref[pl.ds(q * GROUP, GROUP)] = out.reshape(GROUP, 2 * S, TILE)

    @pl.loop(0, quads)
    def _(q):
        rows = own_ref[pl.ds(q * GROUP, GROUP)].reshape(GROUP * 2 * S, TILE)
        for off in range(1, nt):
            row_copy(off, q).wait()
            rows = rows + recv_ref[off - 1, q].astype(F32)
        echo_ref[pl.ds(q * GROUP, GROUP)] = rows.reshape(GROUP, 2 * S, TILE)
        low = rows.astype(BF16)
        rows_ref[0, q] = low
        for off in range(nt - 1, 0, -1):
            rows_copy(off, q).start()
        backward(me_t * npos + q * GROUP, low)

    @pl.loop(0, quads)
    def _(q):
        for off in range(1, nt):
            rows_copy(off, q).wait()
            backward(partner(me_t, off, nt) * npos + q * GROUP, rows_ref[off, q])

    gath_ref[me_f] = adj_ref[...].astype(BF16)
    sp_copies = []
    for off in range(nf - 1, 0, -1):
        cp = pltpu.make_async_remote_copy(
            src_ref=gath_ref.at[me_f],
            dst_ref=gath_ref.at[me_f],
            send_sem=sp_send.at[off],
            recv_sem=sp_recv.at[off],
            device_id=(partner(me_f, off, nf), me_t),
            device_id_type=MESH,
        )
        cp.start()
        sp_copies.append(cp)
    for cp in sp_copies:
        cp.wait()
    spec_out[...] = gath_ref[...]


def synthesis_kernel(freqs, spec_ref, echo_in, back_hbm, echo_out, out_hbm, back_ref, out_ref, sem):
    me_f = lax.axis_index("freq")
    count, cols = out_hbm.shape[0], out_hbm.shape[2]
    chunks = out_ref.shape[0]
    step_t = count // chunks
    lanes = back_ref.shape[1]
    back_copy = pltpu.make_async_copy(back_hbm.at[me_f], back_ref, sem.at[0])
    back_copy.start()
    echo_copy = pltpu.make_async_copy(echo_in, echo_out, sem.at[1])
    echo_copy.start()
    diag = lax.broadcasted_iota(jnp.int32, (S, lanes), 1) % S == lax.broadcasted_iota(
        jnp.int32, (S, lanes), 0
    )
    spec = spec_ref[...].reshape(lanes, cols)
    back_copy.wait()
    copies = []
    for n in range(chunks):
        table = back_ref[n * step_t : (n + 1) * step_t].astype(F32)
        spread = jnp.where(diag[None], table[:, None, :], 0.0).astype(BF16)
        out = nn_dot(spread.reshape(step_t * S, lanes), spec) * freqs**-0.5
        out_ref[n] = out.reshape(step_t, S, cols).astype(BF16)
        cp = pltpu.make_async_copy(
            out_ref.at[n], out_hbm.at[pl.ds(n * step_t, step_t)], sem.at[2 + n]
        )
        cp.start()
        copies.append(cp)
    for cp in copies:
        cp.wait()
    echo_copy.wait()


def shards(nf, nt, recorded_seismograms, left_bases, right_bases, rank_classes, owner):
    count, _, cols = recorded_seismograms.shape
    per_device, row_tiles, col_tiles = left_bases.shape[:3]
    assert per_device == 1
    freqs = per_device * nf
    npos = row_tiles // nt
    quads = npos // GROUP
    left = left_bases.reshape(left_bases.shape[1:])
    right = right_bases.reshape(right_bases.shape[1:])
    ahead, back = trig_tables(nf, count, freqs)
    vmem = pl.BlockSpec(memory_space=pltpu.VMEM)
    smem = pl.BlockSpec(memory_space=pltpu.SMEM)
    hbm = pl.BlockSpec(memory_space=pl.ANY)
    dma = pltpu.SemaphoreType.DMA
    block = (GROUP * 2 * S, TILE)
    echo, spec = pl.pallas_call(
        functools.partial(apply_kernel, nf, nt),
        out_shape=(
            jax.ShapeDtypeStruct((npos, 2 * S, TILE), F32),
            jax.ShapeDtypeStruct((freqs, 2 * S, cols), BF16),
        ),
        in_specs=[hbm, hbm, hbm, smem, smem, hbm],
        out_specs=(vmem, vmem),
        scratch_shapes=[
            pltpu.VMEM(recorded_seismograms.shape, BF16),
            pltpu.VMEM(left.shape, BF16),
            pltpu.VMEM(right.shape, BF16),
            pltpu.VMEM(ahead.shape[1:], BF16),
            pltpu.VMEM((freqs * 2 * S, count * S), BF16),
            pltpu.VMEM((freqs, 2 * S, cols), F32),
            pltpu.VMEM((freqs, 2 * S, cols), BF16),
            pltpu.VMEM((nf, 2 * S, cols), BF16),
            pltpu.VMEM((2 * S, cols), BF16),
            pltpu.VMEM((nt - 1, quads) + block, BF16),
            pltpu.VMEM((nt - 1, quads) + block, BF16),
            pltpu.VMEM((npos, 2 * S, TILE), F32),
            pltpu.VMEM((nt, quads) + block, BF16),
            pltpu.VMEM((2 * S, cols), F32),
            pltpu.VMEM((freqs, 2 * S, cols), BF16),
            dma((7,)),
            dma((nf,)),
            dma((nf,)),
            dma((nt - 1, quads)),
            dma((nt - 1, quads)),
            dma((nt - 1, quads)),
            dma((nt - 1, quads)),
            dma((nf,)),
            dma((nf,)),
        ],
        compiler_params=pltpu.CompilerParams(
            collective_id=0, has_side_effects=True, vmem_limit_bytes=40 * 2**20
        ),
        name="apply",
    )(recorded_seismograms, left, right, rank_classes.reshape(-1), owner, ahead)
    chunks = 4
    echo, synth = pl.pallas_call(
        functools.partial(synthesis_kernel, freqs),
        out_shape=(
            jax.ShapeDtypeStruct(echo.shape, F32),
            jax.ShapeDtypeStruct(recorded_seismograms.shape, BF16),
        ),
        in_specs=[vmem, hbm, hbm],
        out_specs=(hbm, hbm),
        scratch_shapes=[
            pltpu.VMEM(back.shape[1:], BF16),
            pltpu.VMEM((chunks, count // chunks, S, cols), BF16),
            dma((2 + chunks,)),
        ],
        compiler_params=pltpu.CompilerParams(vmem_limit_bytes=40 * 2**20),
        name="synthesis",
    )(spec, echo, back)
    return echo.reshape(1, npos, 2, S, TILE), synth


def solution(mesh):
    nf, nt = mesh.shape["freq"], mesh.shape["tile"]
    in_specs = (
        P("freq", None, "tile"),
        P("freq", None, "tile", None, None, None),
        P("freq", None, "tile", None, None, None),
        P("freq", None, "tile"),
        P(),
    )
    out_specs = (P("freq", "tile", None, None, None), P("freq", None, "tile"))
    return jax.shard_map(
        functools.partial(shards, nf, nt),
        mesh=mesh,
        in_specs=in_specs,
        out_specs=out_specs,
        check_vma=False,
    )
```

time: 171 us -> 59.6 us (0.35)
  waiting for transfers between devices: 65.4 us -> 0 us
  Pallas kernels: 0 us -> 49.3 us
  matrix products: 38.3 us -> 0 us
  local copies, waits for them, and re-layouts: 29.3 us -> 9.35 us
  blocking collectives: 14.5 us -> 0 us
  between operations: 14 us -> 0.66 us
  other arithmetic: 9.13 us -> 0 us
    reduce_scatter x2 -> x0, waiting for transfers between devices: 54.7 us -> none  [the longest x1 28.6 us: shards(): lax.psum_scatter(seismogram_fourier_coeffs(recorded_seismograms, spectral...]
    pallas_call x0 -> x2, Pallas kernels: none -> 49.3 us  [the longest x1 46.6 us: shards(): pl.pallas_call(functools.partial(apply_kernel, nf, nt), out_shape=(jax.Sh...]
    dot_general x20 -> x0, matrix products: 38.3 us -> none  [the longest x16 26.3 us: contract(): return jnp.einsum(form, first, second, preferred_element_type=jnp.float32)]
    all_gather x1 -> x0, blocking collectives: 14.5 us -> none  [shards(): piece = lax.all_gather(adjoint, 'freq', axis=0, tiled=True)]
    gather x4 -> x0, local copies, waits for them, and re-layouts: 11.2 us -> none  [the longest x1 5.02 us: shards(): right_piece = jnp.take(right_bases, owner, axis=1)]
    all_gather x1 -> x0, waiting for transfers between devices: 10.7 us -> none  [shards(): lax.all_gather(echo.astype(jnp.bfloat16), 'tile', axis=1, tiled=True)]
    select_n x3 -> x0, other arithmetic: 6.19 us -> none  [the longest x1 6.05 us: shards(): right_piece = jnp.take(right_bases, owner, axis=1)]
    slice x3 -> x0, local copies, waits for them, and re-layouts: 4.27 us -> none  [the longest x1 4.23 us: shards(): right_real, right_imag = (right_bases[:, :, :, 0], right_bases[:, :, :, 1])]
  transfers between devices with their start and end apart: 3 -> 0, of which waited for: 3 -> 0; matrix products, arithmetic and copies ran while one was open for 13% -> 0% of each run, Pallas kernels for 0% -> 0%
where the time goes in v1:
time: 59.6 us; the launch traced here: 59.3 us
  Pallas kernels  49.3 us (83%)
  local copies, waits for them, and re-layouts  9.35 us (16%)
  between operations  0.66 us (1%)
    pallas_call x1, Pallas kernels, shards(): pl.pallas_call(functools.partial(apply_kernel, nf, nt), out_shape=(jax.Sh...  46.6 us
    unnamed x13, local copies, waits for them, and re-layouts  9.21 us
    pallas_call x1, Pallas kernels, shards(): pl.pallas_call(functools.partial(synthesis_kernel, freqs), out_shape=(jax...  2.7 us

profile of v1, /device:TPU:0, one launch (start us, length us, event | category | flops | bytes accessed | tf_op | source)
XLA Modules:
  0.0 59.3 jit_solution(7253407555232942401)
XLA Ops:
  0.6 0.8 %copy.10 = s32[1,64,2]{2,1,0:T(8,128)S(1)} copy(s32[1,64,2]{1,2,0:T(2,128)} %param.10) | data formatting | bytes 1024 | tf_op args[3]
  1.4 0.1 reshape.18.rank_ref
  1.5 0.0 copy-start
  1.5 2.2 %copy-done = bf16[256,16,512]{2,1,0:T(8,128)(2,1)S(1)} copy-done((bf16[256,16,512]{2,1,0:T(8,128)(2,1)S(1)}, bf16[256,16,512]{2,1,0:T(8,128)(2,1)}, u32[]{:S(2)}) %copy-start) | copy-done | bytes 4194328
  3.7 0.0 copy-start.1
  3.7 2.2 %copy-done.1 = bf16[1,64,2,2,32,256]{5,4,3,2,1,0:T(8,128)(2,1)S(1)} copy-done((bf16[1,64,2,2,32,256]{5,4,3,2,1,0:T(8,128)(2,1)S(1)}, bf16[1,64,2,2,32,256]{5,4,3,2,1,0:T(8,128)(2,1)}, u32[]{:S(2)}) %copy-start.1) | copy-done | bytes 4194328
  5.9 0.0 copy-start.2
  5.9 2.2 %copy-done.2 = bf16[1,64,2,2,32,256]{5,4,3,2,1,0:T(8,128)(2,1)S(1)} copy-done((bf16[1,64,2,2,32,256]{5,4,3,2,1,0:T(8,128)(2,1)S(1)}, bf16[1,64,2,2,32,256]{5,4,3,2,1,0:T(8,128)(2,1)}, u32[]{:S(2)}) %copy-start.2) | copy-done | bytes 4194328
  8.1 0.0 copy-start.4
  8.1 1.2 %copy-done.4 = bf16[8,16,4096]{2,1,0:T(8,128)(2,1)S(1)} copy-done((bf16[8,16,4096]{2,1,0:T(8,128)(2,1)S(1)}, bf16[8,16,4096]{2,1,0:T(8,128)(2,1)}, u32[]{:S(2)}) %copy-start.4) | copy-done | bytes 1048600
  9.3 0.0 copy-start.5
  9.3 0.7 %copy-done.5 = s32[64]{0:T(128)S(1)} copy-done((s32[64]{0:T(128)S(1)}, s32[64]{0:T(128)}, u32[]{:S(2)}) %copy-start.5) | copy-done | bytes 280
  10.0 0.0 copy-start.3
  10.0 46.6 %apply.1 = (f32[16,32,256]{2,1,0:T(8,128)S(1)}, bf16[8,32,512]{2,1,0:T(8,128)(2,1)S(1)}) custom-call(bf16[256,16,512]{2,1,0:T(8,128)(2,1)S(1)} %copy-done, bf16[64,2,2,32,256]{4,3,2,1,0:T(8,128)(2,1)S(1)} %bitcast.3, bf16[64,2,2,32,256]{4,3,2,1,0:T(8,128)(2,1)S(1)} %bitcast.4, s32[128]{0:T(128)S(1)} %reshape.18.rank_ref, s32[64]{0:T(128)S(1)} %copy-done.5, ...), custom_call_target="tpu_custom_call" | custom-call | tf_op jit(solution)/shard_map/apply/pallas_call | solution.py:336
  56.6 0.0 copy-done.3
  56.6 2.7 %synthesis.1 = (f32[16,32,256]{2,1,0:T(8,128)}, bf16[256,16,512]{2,1,0:T(8,128)(2,1)}) custom-call(bf16[8,32,512]{2,1,0:T(8,128)(2,1)S(1)} %get-tuple-element.6.spec_ref, f32[16,32,256]{2,1,0:T(8,128)S(1)} %get-tuple-element.7.echo_in, bf16[8,256,256]{2,1,0:T(8,128)(2,1)S(1)} %copy-done.3), custom_call_target="tpu_custom_call" | custom-call | tf_op jit(solution)/shard_map/synthesis/pallas_call | solution.py:376
Async XLA Ops:
  1.5 2.2 %copy-start = (bf16[256,16,512]{2,1,0:T(8,128)(2,1)S(1)}, bf16[256,16,512]{2,1,0:T(8,128)(2,1)}, u32[]{:S(2)}) copy-start(bf16[256,16,512]{2,1,0:T(8,128)(2,1)} %x_hbm.1) | copy-start | bytes 12582916
  3.7 2.2 %copy-start.1 = (bf16[1,64,2,2,32,256]{5,4,3,2,1,0:T(8,128)(2,1)S(1)}, bf16[1,64,2,2,32,256]{5,4,3,2,1,0:T(8,128)(2,1)}, u32[]{:S(2)}) copy-start(bf16[1,64,2,2,32,256]{5,4,3,2,1,0:T(8,128)(2,1)} %param.8) | copy-start | bytes 12582916
  5.9 2.2 %copy-start.2 = (bf16[1,64,2,2,32,256]{5,4,3,2,1,0:T(8,128)(2,1)S(1)}, bf16[1,64,2,2,32,256]{5,4,3,2,1,0:T(8,128)(2,1)}, u32[]{:S(2)}) copy-start(bf16[1,64,2,2,32,256]{5,4,3,2,1,0:T(8,128)(2,1)} %param.9) | copy-start | bytes 12582916
  8.1 1.2 %copy-start.4 = (bf16[8,16,4096]{2,1,0:T(8,128)(2,1)S(1)}, bf16[8,16,4096]{2,1,0:T(8,128)(2,1)}, u32[]{:S(2)}) copy-start(bf16[8,16,4096]{2,1,0:T(8,128)(2,1)} %constant.4.clone.ahead_hbm) | copy-start | bytes 3145732
  9.3 0.7 %copy-start.5 = (s32[64]{0:T(128)S(1)}, s32[64]{0:T(128)}, u32[]{:S(2)}) copy-start(s32[64]{0:T(128)} %owner_ref.1) | copy-start | bytes 772
  10.0 46.6 %copy-start.3 = (bf16[8,256,256]{2,1,0:T(8,128)(2,1)S(1)}, bf16[8,256,256]{2,1,0:T(8,128)(2,1)}, u32[]{:S(2)}) copy-start(bf16[8,256,256]{2,1,0:T(8,128)(2,1)} %constant.5.clone.back_hbm) | copy-start | bytes 3145732

commit v2 on v1

--- a/solution.py
+++ b/solution.py
@@ -27,7 +27,9 @@
     )
     both = np.stack([np.cos(angles), -np.sin(angles)], 1)
     both = both.reshape(2 * freqs, shards, count)
-    ahead = np.repeat(both.transpose(1, 0, 2), S, axis=2)
+    near = both.reshape(freqs // 2, 2, 2, shards, count).swapaxes(0, 1)
+    near = near.reshape(2 * freqs, shards, count)
+    ahead = np.repeat(near.transpose(1, 0, 2), S, axis=2)
     back = np.repeat(both.transpose(1, 2, 0), S, axis=2)
     return jnp.asarray(ahead, BF16), jnp.asarray(back, BF16)
 
@@ -68,15 +70,18 @@
     a_ref,
     acc_ref,
     part_ref,
+    pair_ref,
     rs_ref,
     s_ref,
     send_ref,
     recv_ref,
+    mid_ref,
     own_ref,
     rows_ref,
     adj_ref,
     gath_ref,
     load_sem,
+    pair_sem,
     rs_send,
     rs_recv,
     row_send,
@@ -88,10 +93,13 @@
 ):
     me_f = lax.axis_index("freq")
     me_t = lax.axis_index("tile")
+    nz = nf // 2
+    me_z, core = me_f // 2, me_f % 2
+    sibling = me_f + 1 - 2 * core
     count = x_ref.shape[0]
     cols = x_ref.shape[2]
     col_tiles = l_ref.shape[1]
-    freqs = part_ref.shape[0]
+    freqs = nf
     npos = own_ref.shape[0]
     quads = npos // GROUP
     chunks = 4
@@ -113,11 +121,18 @@
     l_copy.start()
 
     barrier = pltpu.get_barrier_semaphore()
-    for off in range(1, nf):
+    pl.semaphore_signal(barrier, inc=1, device_id=(sibling, me_t), device_id_type=MESH)
+    for off in range(1, nz):
         pl.semaphore_signal(
-            barrier, inc=1, device_id=(partner(me_f, off, nf), me_t), device_id_type=MESH
-        )
-    for off in range(1, nt):
+            barrier,
+            inc=1,
+            device_id=(2 * partner(me_z, off, nz) + core, me_t),
+            device_id_type=MESH,
+        )
+    two_level = nt == 4 and quads % 2 == 0
+    offsets = (1, 2) if two_level else range(1, nt)
+    barrier_count = nz + len(offsets)
+    for off in offsets:
         pl.semaphore_signal(
             barrier, inc=1, device_id=(me_f, partner(me_t, off, nt)), device_id_type=MESH
         )
@@ -126,6 +141,7 @@
     diag = lax.broadcasted_iota(jnp.int32, (S, kk), 1) % S == lax.broadcasted_iota(
         jnp.int32, (S, kk), 0
     )
+    total = 0.0
     for n in range(chunks):
         table = ahead_ref[:, n * kk : (n + 1) * kk].astype(F32)
         for k in range(2 * freqs):
@@ -133,32 +149,45 @@
             a_ref[k * S : (k + 1) * S, n * kk : (n + 1) * kk] = jnp.where(diag, row, 0.0).astype(
                 BF16
             )
-    for n in range(chunks):
         x_copies[n].wait()
-    total = nn_dot(a_ref[...], x_ref[...].reshape(count * S, cols)) * RECORD_LENGTH**-0.5
-    total = total.reshape(freqs, 2 * S, cols)
+        block_x = x_ref[n * step_t : (n + 1) * step_t].reshape(kk, cols)
+        total = total + nn_dot(a_ref[:, n * kk : (n + 1) * kk], block_x)
+    total = (total * RECORD_LENGTH**-0.5).reshape(2, nz, 2 * S, cols)
     acc_ref[...] = total
     part_ref[...] = total.astype(BF16)
 
-    pl.semaphore_wait(barrier, nf + nt - 2)
+    pl.semaphore_wait(barrier, barrier_count)
+    pair_copy = pltpu.make_async_remote_copy(
+        src_ref=part_ref.at[1 - core],
+        dst_ref=pair_ref,
+        send_sem=pair_sem.at[0],
+        recv_sem=pair_sem.at[1],
+        device_id=(sibling, me_t),
+        device_id_type=MESH,
+    )
+    pair_copy.start()
+    adj_ref[...] = jnp.zeros_like(adj_ref)
+    r_copy.wait()
+    l_copy.wait()
+    pair_copy.wait()
+    summed = acc_ref[core] + pair_ref[...].astype(F32)
+    acc_ref[core] = summed
+    part_ref[core] = summed.astype(BF16)
     rs_copies = []
-    for off in range(nf - 1, 0, -1):
-        to = partner(me_f, off, nf)
+    for off in range(nz - 1, 0, -1):
+        to = partner(me_z, off, nz)
         cp = pltpu.make_async_remote_copy(
-            src_ref=part_ref.at[to],
+            src_ref=part_ref.at[core, to],
             dst_ref=rs_ref.at[off],
             send_sem=rs_send.at[off],
             recv_sem=rs_recv.at[off],
-            device_id=(to, me_t),
+            device_id=(2 * to + core, me_t),
             device_id_type=MESH,
         )
         cp.start()
         rs_copies.append((off, cp))
-    adj_ref[...] = jnp.zeros_like(adj_ref)
-    r_copy.wait()
-    l_copy.wait()
-    spectra = acc_ref[me_f]
-    for off, cp in rs_copies:
+    spectra = acc_ref[core, me_z]
+    for off, cp in reversed(rs_copies):
         cp.wait()
         spectra = spectra + rs_ref[off].astype(F32)
     s_ref[...] = spectra.astype(BF16)
@@ -178,7 +207,7 @@
     def kept(idx, j):
         limit = jnp.zeros((1, width), jnp.int32)
         for m, i in enumerate(idx):
-            value = (rank_ref[i * col_tiles + j] + 1) * (RMAX // 4)
+            value = (rank_ref[j, i] + 1) * (RMAX // 4)
             limit = jnp.where(lane_m == m, value, limit)
         return jnp.where(lane_r < limit, 1.0, 0.0).astype(F32)
 
@@ -241,48 +270,136 @@
             device_id_type=MESH,
         )
 
-    @pl.loop(0, quads)
-    def _(q):
-        for off in range(nt - 1, 0, -1):
-            out = forward(partner(me_t, off, nt) * npos + q * GROUP)
-            send_ref[off - 1, q] = out.astype(BF16)
-            row_copy(off, q).start()
-        out = forward(me_t * npos + q * GROUP)
-        own_ref[pl.ds(q * GROUP, GROUP)] = out.reshape(GROUP, 2 * S, TILE)
-
-    @pl.loop(0, quads)
-    def _(q):
-        rows = own_ref[pl.ds(q * GROUP, GROUP)].reshape(GROUP * 2 * S, TILE)
-        for off in range(1, nt):
-            row_copy(off, q).wait()
-            rows = rows + recv_ref[off - 1, q].astype(F32)
-        echo_ref[pl.ds(q * GROUP, GROUP)] = rows.reshape(GROUP, 2 * S, TILE)
-        low = rows.astype(BF16)
-        rows_ref[0, q] = low
-        for off in range(nt - 1, 0, -1):
-            rows_copy(off, q).start()
-        backward(me_t * npos + q * GROUP, low)
-
-    @pl.loop(0, quads)
-    def _(q):
-        for off in range(1, nt):
-            rows_copy(off, q).wait()
-            backward(partner(me_t, off, nt) * npos + q * GROUP, rows_ref[off, q])
+    if two_level:
+
+        def hop(src, dst, sems, k, q, off):
+            return pltpu.make_async_remote_copy(
+                src_ref=src,
+                dst_ref=dst,
+                send_sem=sems[0].at[k, q],
+                recv_sem=sems[1].at[k, q],
+                device_id=(me_f, partner(me_t, off, nt)),
+                device_id_type=MESH,
+            )
+
+        def row_hop(k, q, off):
+            return hop(send_ref.at[k, q], recv_ref.at[k, q], (row_send, row_recv), k, q, off)
+
+        def ag_hop(k, q, src, off):
+            return hop(rows_ref.at[src, q], rows_ref.at[k, q], (ag_send, ag_recv), k - 1, q, off)
+
+        def base_of(off, q):
+            return partner(me_t, off, nt) * npos + q * GROUP
+
+        @pl.loop(0, quads // 2)
+        def _(half):
+            for k in range(2):
+                for first in (1, 2):
+                    q = 2 * half + first - 1
+                    off = (3, first)[k]
+                    send_ref[k, q] = forward(base_of(off, q)).astype(BF16)
+                    row_hop(k, q, first).start()
+            for first in (1, 2):
+                q = 2 * half + first - 1
+                mid_ref[q] = forward(base_of(3 - first, q))
+                out = forward(base_of(0, q))
+                own_ref[pl.ds(q * GROUP, GROUP)] = out.reshape(GROUP, 2 * S, TILE)
+
+        @pl.loop(0, quads // 2)
+        def _(half):
+            for first in (1, 2):
+                q = 2 * half + first - 1
+                row_hop(0, q, first).wait()
+                send_ref[2, q] = (mid_ref[q] + recv_ref[0, q].astype(F32)).astype(BF16)
+                row_hop(2, q, 3 - first).start()
+
+        @pl.loop(0, quads // 2)
+        def _(half):
+            for first in (1, 2):
+                q = 2 * half + first - 1
+                rows = own_ref[pl.ds(q * GROUP, GROUP)].reshape(GROUP * 2 * S, TILE)
+                row_hop(1, q, first).wait()
+                row_hop(2, q, 3 - first).wait()
+                rows = rows + recv_ref[1, q].astype(F32) + recv_ref[2, q].astype(F32)
+                echo_ref[pl.ds(q * GROUP, GROUP)] = rows.reshape(GROUP, 2 * S, TILE)
+                low = rows.astype(BF16)
+                rows_ref[0, q] = low
+                ag_hop(first, q, 0, first).start()
+                ag_hop(3 - first, q, 0, 3 - first).start()
+                backward(base_of(0, q), low)
+
+        @pl.loop(0, quads // 2)
+        def _(half):
+            for first in (1, 2):
+                q = 2 * half + first - 1
+                ag_hop(first, q, 0, first).wait()
+                ag_hop(3, q, first, 3 - first).start()
+                ag_hop(3 - first, q, 0, 3 - first).wait()
+                backward(base_of(first, q), rows_ref[first, q])
+                backward(base_of(3 - first, q), rows_ref[3 - first, q])
+
+        @pl.loop(0, quads // 2)
+        def _(half):
+            for first in (1, 2):
+                q = 2 * half + first - 1
+                ag_hop(3, q, first, 3 - first).wait()
+                backward(base_of(3, q), rows_ref[3, q])
+
+    else:
+
+        @pl.loop(0, quads)
+        def _(q):
+            for off in range(nt - 1, 0, -1):
+                out = forward(partner(me_t, off, nt) * npos + q * GROUP)
+                send_ref[off - 1, q] = out.astype(BF16)
+                row_copy(off, q).start()
+            out = forward(me_t * npos + q * GROUP)
+            own_ref[pl.ds(q * GROUP, GROUP)] = out.reshape(GROUP, 2 * S, TILE)
+
+        @pl.loop(0, quads)
+        def _(q):
+            rows = own_ref[pl.ds(q * GROUP, GROUP)].reshape(GROUP * 2 * S, TILE)
+            for off in range(1, nt):
+                row_copy(off, q).wait()
+                rows = rows + recv_ref[off - 1, q].astype(F32)
+            echo_ref[pl.ds(q * GROUP, GROUP)] = rows.reshape(GROUP, 2 * S, TILE)
+            low = rows.astype(BF16)
+            rows_ref[0, q] = low
+            for off in range(nt - 1, 0, -1):
+                rows_copy(off, q).start()
+            backward(me_t * npos + q * GROUP, low)
+
+        @pl.loop(0, quads)
+        def _(q):
+            for off in range(1, nt):
+                rows_copy(off, q).wait()
+                backward(partner(me_t, off, nt) * npos + q * GROUP, rows_ref[off, q])
 
     gath_ref[me_f] = adj_ref[...].astype(BF16)
+
+    def spec_copy(n, at, to):
+        return pltpu.make_async_remote_copy(
+            src_ref=gath_ref.at[at],
+            dst_ref=gath_ref.at[at],
+            send_sem=sp_send.at[n],
+            recv_sem=sp_recv.at[n],
+            device_id=(to, me_t),
+            device_id_type=MESH,
+        )
+
     sp_copies = []
-    for off in range(nf - 1, 0, -1):
-        cp = pltpu.make_async_remote_copy(
-            src_ref=gath_ref.at[me_f],
-            dst_ref=gath_ref.at[me_f],
-            send_sem=sp_send.at[off],
-            recv_sem=sp_recv.at[off],
-            device_id=(partner(me_f, off, nf), me_t),
-            device_id_type=MESH,
-        )
+    for off in range(nz - 1, 0, -1):
+        to = 2 * partner(me_z, off, nz) + core
+        cp = spec_copy(off, me_f, to)
         cp.start()
-        sp_copies.append(cp)
-    for cp in sp_copies:
+        sp_copies.append((off, to, cp))
+    last = [spec_copy(nz, me_f, sibling)]
+    last[0].start()
+    for off, to, cp in reversed(sp_copies):
+        cp.wait()
+        last.append(spec_copy(nz + off, to, sibling))
+        last[-1].start()
+    for cp in last:
         cp.wait()
     spec_out[...] = gath_ref[...]
 
@@ -330,7 +447,7 @@
     ahead, back = trig_tables(nf, count, freqs)
     vmem = pl.BlockSpec(memory_space=pltpu.VMEM)
     smem = pl.BlockSpec(memory_space=pltpu.SMEM)
-    hbm = pl.BlockSpec(memory_space=pl.ANY)
+    hbm = pl.BlockSpec(memory_space=pltpu.HBM)
     dma = pltpu.SemaphoreType.DMA
     block = (GROUP * 2 * S, TILE)
     echo, spec = pl.pallas_call(
@@ -347,17 +464,20 @@
             pltpu.VMEM(right.shape, BF16),
             pltpu.VMEM(ahead.shape[1:], BF16),
             pltpu.VMEM((freqs * 2 * S, count * S), BF16),
-            pltpu.VMEM((freqs, 2 * S, cols), F32),
-            pltpu.VMEM((freqs, 2 * S, cols), BF16),
-            pltpu.VMEM((nf, 2 * S, cols), BF16),
+            pltpu.VMEM((2, nf // 2, 2 * S, cols), F32),
+            pltpu.VMEM((2, nf // 2, 2 * S, cols), BF16),
+            pltpu.VMEM((nf // 2, 2 * S, cols), BF16),
+            pltpu.VMEM((nf // 2, 2 * S, cols), BF16),
             pltpu.VMEM((2 * S, cols), BF16),
             pltpu.VMEM((nt - 1, quads) + block, BF16),
             pltpu.VMEM((nt - 1, quads) + block, BF16),
+            pltpu.VMEM((quads,) + block, F32),
             pltpu.VMEM((npos, 2 * S, TILE), F32),
             pltpu.VMEM((nt, quads) + block, BF16),
             pltpu.VMEM((2 * S, cols), F32),
             pltpu.VMEM((freqs, 2 * S, cols), BF16),
             dma((7,)),
+            dma((2,)),
             dma((nf,)),
             dma((nf,)),
             dma((nt - 1, quads)),
@@ -368,10 +488,10 @@
             dma((nf,)),
         ],
         compiler_params=pltpu.CompilerParams(
-            collective_id=0, has_side_effects=True, vmem_limit_bytes=40 * 2**20
+            collective_id=0, has_side_effects=True, vmem_limit_bytes=60 * 2**20
         ),
         name="apply",
-    )(recorded_seismograms, left, right, rank_classes.reshape(-1), owner, ahead)
+    )(recorded_seismograms, left, right, rank_classes[0].T, owner, ahead)
     chunks = 4
     echo, synth = pl.pallas_call(
         functools.partial(synthesis_kernel, freqs),
@@ -379,14 +499,14 @@
             jax.ShapeDtypeStruct(echo.shape, F32),
             jax.ShapeDtypeStruct(recorded_seismograms.shape, BF16),
         ),
-        in_specs=[vmem, hbm, hbm],
+        in_specs=[vmem, vmem, hbm],
         out_specs=(hbm, hbm),
         scratch_shapes=[
             pltpu.VMEM(back.shape[1:], BF16),
             pltpu.VMEM((chunks, count // chunks, S, cols), BF16),
             dma((2 + chunks,)),
         ],
-        compiler_params=pltpu.CompilerParams(vmem_limit_bytes=40 * 2**20),
+        compiler_params=pltpu.CompilerParams(vmem_limit_bytes=60 * 2**20),
         name="synthesis",
     )(spec, echo, back)
     return echo.reshape(1, npos, 2, S, TILE), synth

time: 59.6 us -> 46.9 us (0.79)
  local copies, waits for them, and re-layouts: 9.35 us -> 0 us
  Pallas kernels: 49.3 us -> 46.1 us
    unnamed x13 -> x0, local copies, waits for them, and re-layouts: 9.21 us -> none
    pallas_call x1, Pallas kernels: 46.6 us -> 41.4 us  [shards(): pl.pallas_call(functools.partial(apply_kernel, nf, nt), out_shape=(jax.Sh...]
    pallas_call x1, Pallas kernels: 2.7 us -> 4.66 us  [shards(): pl.pallas_call(functools.partial(synthesis_kernel, freqs), out_shape=(jax...]
where the time goes in v2:
time: 46.9 us; the launch traced here: 46.7 us
  Pallas kernels  46.1 us (98%)
  between operations  0.64 us (1%)
    pallas_call x1, Pallas kernels, shards(): pl.pallas_call(functools.partial(apply_kernel, nf, nt), out_shape=(jax.Sh...  41.4 us
    pallas_call x1, Pallas kernels, shards(): pl.pallas_call(functools.partial(synthesis_kernel, freqs), out_shape=(jax...  4.66 us

profile of v2, /device:TPU:0, one launch (start us, length us, event | category | flops | bytes accessed | tf_op | source)
XLA Modules:
  0.0 46.7 jit_solution(11824927481511956351)
XLA Ops:
  0.6 41.4 %apply.1 = (f32[16,32,256]{2,1,0:T(8,128)}, bf16[8,32,512]{2,1,0:T(8,128)(2,1)}) custom-call(bf16[256,16,512]{2,1,0:T(8,128)(2,1)} %x_hbm.1, bf16[64,2,2,32,256]{4,3,2,1,0:T(8,128)(2,1)} %bitcast.6, bf16[64,2,2,32,256]{4,3,2,1,0:T(8,128)(2,1)} %bitcast.7, s32[2,64]{1,0:T(2,128)} %bitcast.8, s32[64]{0:T(128)} %owner_ref.1, ...), custom_call_target="tpu_custom_call" | custom-call | tf_op jit(solution)/shard_map/apply/pallas_call | solution.py:453
  42.1 4.7 %synthesis.1 = (f32[16,32,256]{2,1,0:T(8,128)}, bf16[256,16,512]{2,1,0:T(8,128)(2,1)}) custom-call(bf16[8,32,512]{2,1,0:T(8,128)(2,1)} %get-tuple-element.6.spec_ref, f32[16,32,256]{2,1,0:T(8,128)} %get-tuple-element.7.echo_in, bf16[8,256,256]{2,1,0:T(8,128)(2,1)} %constant.5.clone.back_hbm), custom_call_target="tpu_custom_call" | custom-call | tf_op jit(solution)/shard_map/synthesis/pallas_call | solution.py:496

commit v3 on v2

--- a/solution.py
+++ b/solution.py
@@ -75,7 +75,6 @@
     s_ref,
     send_ref,
     recv_ref,
-    mid_ref,
     own_ref,
     rows_ref,
     adj_ref,
@@ -116,9 +115,7 @@
         cp.start()
         x_copies.append(cp)
     r_copy = pltpu.make_async_copy(r_hbm, r_ref, load_sem.at[1 + chunks])
-    r_copy.start()
     l_copy = pltpu.make_async_copy(l_hbm, l_ref, load_sem.at[2 + chunks])
-    l_copy.start()
 
     barrier = pltpu.get_barrier_semaphore()
     pl.semaphore_signal(barrier, inc=1, device_id=(sibling, me_t), device_id_type=MESH)
@@ -150,6 +147,9 @@
                 BF16
             )
         x_copies[n].wait()
+        if n == chunks - 2:
+            r_copy.start()
+            l_copy.start()
         block_x = x_ref[n * step_t : (n + 1) * step_t].reshape(kk, cols)
         total = total + nn_dot(a_ref[:, n * kk : (n + 1) * kk], block_x)
     total = (total * RECORD_LENGTH**-0.5).reshape(2, nz, 2 * S, cols)
@@ -167,8 +167,6 @@
     )
     pair_copy.start()
     adj_ref[...] = jnp.zeros_like(adj_ref)
-    r_copy.wait()
-    l_copy.wait()
     pair_copy.wait()
     summed = acc_ref[core] + pair_ref[...].astype(F32)
     acc_ref[core] = summed
@@ -191,6 +189,8 @@
         cp.wait()
         spectra = spectra + rs_ref[off].astype(F32)
     s_ref[...] = spectra.astype(BF16)
+    r_copy.wait()
+    l_copy.wait()
 
     width = GROUP * RMAX
     lane = lax.broadcasted_iota(jnp.int32, (1, width), 1)
@@ -293,25 +293,30 @@
 
         @pl.loop(0, quads // 2)
         def _(half):
-            for k in range(2):
-                for first in (1, 2):
-                    q = 2 * half + first - 1
-                    off = (3, first)[k]
-                    send_ref[k, q] = forward(base_of(off, q)).astype(BF16)
-                    row_hop(k, q, first).start()
-            for first in (1, 2):
-                q = 2 * half + first - 1
-                mid_ref[q] = forward(base_of(3 - first, q))
+            for first in (1, 2):
+                q = 2 * half + first - 1
+                send_ref[0, q] = forward(base_of(3, q)).astype(BF16)
+                row_hop(0, q, first).start()
+
+        @pl.loop(0, quads // 2)
+        def _(half):
+            for first in (1, 2):
+                q = 2 * half + first - 1
+                send_ref[1, q] = forward(base_of(first, q)).astype(BF16)
+                row_hop(1, q, first).start()
+            for first in (1, 2):
+                q = 2 * half + first - 1
+                mid = forward(base_of(3 - first, q))
+                row_hop(0, q, first).wait()
+                send_ref[2, q] = (mid + recv_ref[0, q].astype(F32)).astype(BF16)
+                row_hop(2, q, 3 - first).start()
+
+        @pl.loop(0, quads // 2)
+        def _(half):
+            for first in (1, 2):
+                q = 2 * half + first - 1
                 out = forward(base_of(0, q))
                 own_ref[pl.ds(q * GROUP, GROUP)] = out.reshape(GROUP, 2 * S, TILE)
-
-        @pl.loop(0, quads // 2)
-        def _(half):
-            for first in (1, 2):
-                q = 2 * half + first - 1
-                row_hop(0, q, first).wait()
-                send_ref[2, q] = (mid_ref[q] + recv_ref[0, q].astype(F32)).astype(BF16)
-                row_hop(2, q, 3 - first).start()
 
         @pl.loop(0, quads // 2)
         def _(half):
@@ -404,7 +409,9 @@
     spec_out[...] = gath_ref[...]
 
 
-def synthesis_kernel(freqs, spec_ref, echo_in, back_hbm, echo_out, out_hbm, back_ref, out_ref, sem):
+def synthesis_kernel(
+    freqs, spec_hbm, echo_in, back_hbm, echo_out, out_hbm, spec_ref, echo_ref, back_ref, out_ref, sem
+):
     me_f = lax.axis_index("freq")
     count, cols = out_hbm.shape[0], out_hbm.shape[2]
     chunks = out_ref.shape[0]
@@ -412,13 +419,16 @@
     lanes = back_ref.shape[1]
     back_copy = pltpu.make_async_copy(back_hbm.at[me_f], back_ref, sem.at[0])
     back_copy.start()
-    echo_copy = pltpu.make_async_copy(echo_in, echo_out, sem.at[1])
-    echo_copy.start()
+    spec_copy = pltpu.make_async_copy(spec_hbm, spec_ref, sem.at[1])
+    spec_copy.start()
+    echo_load = pltpu.make_async_copy(echo_in, echo_ref, sem.at[2])
+    echo_load.start()
     diag = lax.broadcasted_iota(jnp.int32, (S, lanes), 1) % S == lax.broadcasted_iota(
         jnp.int32, (S, lanes), 0
     )
+    back_copy.wait()
+    spec_copy.wait()
     spec = spec_ref[...].reshape(lanes, cols)
-    back_copy.wait()
     copies = []
     for n in range(chunks):
         table = back_ref[n * step_t : (n + 1) * step_t].astype(F32)
@@ -426,10 +436,13 @@
         out = nn_dot(spread.reshape(step_t * S, lanes), spec) * freqs**-0.5
         out_ref[n] = out.reshape(step_t, S, cols).astype(BF16)
         cp = pltpu.make_async_copy(
-            out_ref.at[n], out_hbm.at[pl.ds(n * step_t, step_t)], sem.at[2 + n]
+            out_ref.at[n], out_hbm.at[pl.ds(n * step_t, step_t)], sem.at[4 + n]
         )
         cp.start()
         copies.append(cp)
+    echo_load.wait()
+    echo_copy = pltpu.make_async_copy(echo_ref, echo_out, sem.at[3])
+    echo_copy.start()
     for cp in copies:
         cp.wait()
     echo_copy.wait()
@@ -471,7 +484,6 @@
             pltpu.VMEM((2 * S, cols), BF16),
             pltpu.VMEM((nt - 1, quads) + block, BF16),
             pltpu.VMEM((nt - 1, quads) + block, BF16),
-            pltpu.VMEM((quads,) + block, F32),
             pltpu.VMEM((npos, 2 * S, TILE), F32),
             pltpu.VMEM((nt, quads) + block, BF16),
             pltpu.VMEM((2 * S, cols), F32),
@@ -492,19 +504,21 @@
         ),
         name="apply",
     )(recorded_seismograms, left, right, rank_classes[0].T, owner, ahead)
-    chunks = 4
+    chunks = 8
     echo, synth = pl.pallas_call(
         functools.partial(synthesis_kernel, freqs),
         out_shape=(
             jax.ShapeDtypeStruct(echo.shape, F32),
             jax.ShapeDtypeStruct(recorded_seismograms.shape, BF16),
         ),
-        in_specs=[vmem, vmem, hbm],
+        in_specs=[hbm, hbm, hbm],
         out_specs=(hbm, hbm),
         scratch_shapes=[
+            pltpu.VMEM(spec.shape, BF16),
+            pltpu.VMEM(echo.shape, F32),
             pltpu.VMEM(back.shape[1:], BF16),
             pltpu.VMEM((chunks, count // chunks, S, cols), BF16),
-            dma((2 + chunks,)),
+            dma((4 + chunks,)),
         ],
         compiler_params=pltpu.CompilerParams(vmem_limit_bytes=60 * 2**20),
         name="synthesis",

time: 46.9 us -> 45.6 us (0.972)
  Pallas kernels: 46.1 us -> 44.8 us
    pallas_call x1, Pallas kernels: 4.66 us -> 3.61 us  [shards(): pl.pallas_call(functools.partial(synthesis_kernel, freqs), out_shape=(jax...]
where the time goes in v3:
time: 45.6 us; the launch traced here: 45.5 us
  Pallas kernels  44.8 us (98%)
  between operations  0.64 us (1%)
    pallas_call x1, Pallas kernels, shards(): pl.pallas_call(functools.partial(apply_kernel, nf, nt), out_shape=(jax.Sh...  41.2 us
    pallas_call x1, Pallas kernels, shards(): pl.pallas_call(functools.partial(synthesis_kernel, freqs), out_shape=(jax...  3.61 us

profile of v3, /device:TPU:0, one launch (start us, length us, event | category | flops | bytes accessed | tf_op | source)
XLA Modules:
  0.0 45.5 jit_solution(13104587576896116175)
XLA Ops:
  0.6 41.2 %apply.1 = (f32[16,32,256]{2,1,0:T(8,128)}, bf16[8,32,512]{2,1,0:T(8,128)(2,1)}) custom-call(bf16[256,16,512]{2,1,0:T(8,128)(2,1)} %x_hbm.1, bf16[64,2,2,32,256]{4,3,2,1,0:T(8,128)(2,1)} %bitcast.6, bf16[64,2,2,32,256]{4,3,2,1,0:T(8,128)(2,1)} %bitcast.7, s32[2,64]{1,0:T(2,128)} %bitcast.8, s32[64]{0:T(128)} %owner_ref.1, ...), custom_call_target="tpu_custom_call" | custom-call | tf_op jit(solution)/shard_map/apply/pallas_call | solution.py:466
  41.8 3.6 %synthesis.1 = (f32[16,32,256]{2,1,0:T(8,128)}, bf16[256,16,512]{2,1,0:T(8,128)(2,1)}) custom-call(bf16[8,32,512]{2,1,0:T(8,128)(2,1)} %get-tuple-element.6.spec_hbm, f32[16,32,256]{2,1,0:T(8,128)} %get-tuple-element.7.echo_in, bf16[8,256,256]{2,1,0:T(8,128)(2,1)} %constant.5.clone.back_hbm), custom_call_target="tpu_custom_call" | custom-call | tf_op jit(solution)/shard_map/synthesis/pallas_call | solution.py:508
